TPU v7x, 128 devices: a whole 4x4x4 slice. The times are simulated.
128 devices in a mesh: sess: 16 (over y_lo, z, core), tp: 8 (over y_hi, x).
Axes of the slice: x: 4, y: 4 (y_hi: 2, y_lo: 2; y = y_hi * 2 + y_lo), z: 4, core: 2. Of those that a mesh axis runs over, the one named last changes fastest.
Arguments:
- x_resid: bfloat16 [256, 8192], P(None, 'sess'), may hold values from -18 to 18
- qkv_new: bfloat16 [256, 8, 1280], P('sess', 'tp'), may hold values from -60 to 60
- kv_cache: bfloat16 [256, 2, 8, 1024, 128], P('sess', None, 'tp'), may hold values from -8 to 8
- cache_lens: int32 [256], P('sess'), may hold values from 1 to 1024, as said below
- wo_temporal: bfloat16 [8192, 8192], P('tp', 'sess'), may hold values from -0.0625 to 0.0625
- norm_gain: float32 [8192], P('sess'), may hold values from 0.1 to 1.9
- w_in: bfloat16 [8, 8192, 1024], P('tp', 'sess'), may hold values from -0.0625 to 0.0625
- embed_rows: bfloat16 [8, 2048, 1024], P('tp', 'sess'), may hold values from -6 to 6
- token_ids: int32 [256, 8], P(None, 'tp'), may hold values from 0 to 2047
- depth_gain: float32 [8, 1024], P('tp'), may hold values from 0.1 to 1.9
- depth_qkv: bfloat16 [8, 1024, 3072], P('tp'), may hold values from -6 to 6
- depth_out: bfloat16 [8, 1024, 1024], P('tp'), may hold values from -0.1875 to 0.1875
Outputs:
- depth_hidden: bfloat16 [256, 8, 1024], P('sess', 'tp')
Inputs may be any that keep to these rules, and one draw needn't show every extreme that they name: `cache_lens`: some session has exactly 1024 live frames.
All inputs are finite; a program needn't handle non-finite values.
Results may differ from a plain program's by a relative error of at most 0.009.
Values may be sent and summed in bfloat16 or wider, within the bound.
A program may use at most 64 MiB of HBM per device.

v0:
```python
import jax
import jax.numpy as jnp
from jax import lax
from jax.sharding import PartitionSpec as P

D = 8192
DHEADS = 16
EPS = 1e-05


def temporal_attention(qkv_new, kv_cache, cache_lens):
    sess_rows = kv_cache.shape[0]
    kv_local = kv_cache.shape[2]
    cache_frames = kv_cache.shape[3]
    head_size = kv_cache.shape[4]
    group = qkv_new.shape[2] // head_size - 2
    queries = qkv_new[:, :, : group * head_size].reshape(sess_rows, kv_local, group, head_size)
    new_key = qkv_new[:, :, group * head_size : (group + 1) * head_size]
    new_value = qkv_new[:, :, (group + 1) * head_size :]
    score_scale = head_size ** (-0.5)
    old_scores = (
        jnp.einsum("skgd,skld->skgl", queries, kv_cache[:, 0], preferred_element_type=jnp.float32)
        * score_scale
    )
    new_scores = (
        jnp.einsum("skgd,skd->skg", queries, new_key, preferred_element_type=jnp.float32)
        * score_scale
    )
    frames = lax.broadcasted_iota(jnp.int32, (1, 1, 1, cache_frames), 3)
    visible = frames < cache_lens[:, None, None, None]
    peak_score = jnp.maximum(jnp.max(jnp.where(visible, old_scores, -1e30), axis=-1), new_scores)
    old_exp = jnp.where(visible, jnp.exp(old_scores - peak_score[..., None]), 0.0)
    new_exp = jnp.exp(new_scores - peak_score)
    summed_exp = jnp.sum(old_exp, axis=-1) + new_exp
    old_weights = (old_exp / summed_exp[..., None]).astype(jnp.bfloat16)
    new_weights = (new_exp / summed_exp).astype(jnp.bfloat16)
    context = jnp.einsum(
        "skgl,skld->skgd", old_weights, kv_cache[:, 1], preferred_element_type=jnp.float32
    )
    context = (
        context
        + new_weights.astype(jnp.float32)[..., None] * new_value.astype(jnp.float32)[:, :, None, :]
    )
    return context.astype(jnp.bfloat16).reshape(sess_rows, kv_local * group * head_size)


def normalize_rows(hidden, squares, norm_gain):
    scaled = hidden * lax.rsqrt(squares / D + EPS)[:, None] * norm_gain[None, :]
    return scaled.astype(jnp.bfloat16)


def shards(
    x_resid,
    qkv_new,
    kv_cache,
    cache_lens,
    wo_temporal,
    norm_gain,
    w_in,
    embed_rows,
    token_ids,
    depth_gain,
    depth_qkv,
    depth_out,
):
    sess_rows = kv_cache.shape[0]
    attn_rows = temporal_attention(qkv_new, kv_cache, cache_lens)
    partial_out = jnp.dot(
        lax.all_gather(attn_rows, "sess", axis=0, tiled=True),
        wo_temporal,
        preferred_element_type=jnp.float32,
    )
    summed = lax.psum(partial_out, "tp")
    hidden = x_resid.astype(jnp.float32) + summed
    squares = lax.psum(jnp.sum(hidden * hidden, axis=1), "sess")
    normed = normalize_rows(hidden, squares, norm_gain)
    cb_local = w_in.shape[0]
    depth_width = w_in.shape[2]
    vocab_rows = embed_rows.shape[1]
    vocab_start = lax.axis_index("sess") * vocab_rows
    vocab_iota = lax.broadcasted_iota(jnp.int32, (1, 1, vocab_rows), 2)
    projected = jnp.einsum("rd,cde->rce", normed, w_in, preferred_element_type=jnp.float32)
    one_hot = (token_ids[:, :, None] - vocab_start == vocab_iota).astype(jnp.bfloat16)
    looked = jnp.einsum("rcv,cve->rce", one_hot, embed_rows, preferred_element_type=jnp.float32)
    depth_flat = lax.psum_scatter(
        (projected + looked).reshape(sess_rows * lax.axis_size("sess"), cb_local * depth_width),
        "sess",
        scatter_dimension=0,
        tiled=True,
    )
    depth_in = depth_flat.reshape(sess_rows, cb_local, depth_width)
    mean_sq = jnp.mean(depth_in * depth_in, axis=-1)
    depth_normed = (depth_in * lax.rsqrt(mean_sq + EPS)[..., None] * depth_gain[None]).astype(
        jnp.bfloat16
    )
    depth_proj = jnp.einsum(
        "sce,cef->scf", depth_normed, depth_qkv, preferred_element_type=jnp.float32
    ).astype(jnp.bfloat16)
    head_size = depth_width // DHEADS
    queries = depth_proj[..., :depth_width].reshape(sess_rows, cb_local, DHEADS, head_size)
    key_values = depth_proj[..., depth_width:]
    owned = lax.axis_index("tp") * cb_local + lax.broadcasted_iota(jnp.int32, (cb_local,), 0)
    score_scale = head_size ** (-0.5)
    start_peak = jnp.full((sess_rows, cb_local, DHEADS), -1e30, jnp.float32)
    block_in = lax.all_gather(key_values, "tp", axis=1, tiled=True)
    positions = block_in.shape[1]
    block_keys = block_in[..., :depth_width].reshape(sess_rows, positions, DHEADS, head_size)
    block_values = block_in[..., depth_width:].reshape(sess_rows, positions, DHEADS, head_size)
    scores = (
        jnp.einsum("schd,snhd->schn", queries, block_keys, preferred_element_type=jnp.float32)
        * score_scale
    )
    key_pos = lax.broadcasted_iota(jnp.int32, (positions,), 0)
    visible = key_pos[None, None, None, :] <= owned[None, :, None, None]
    peak_next = jnp.maximum(start_peak, jnp.max(jnp.where(visible, scores, -1e30), axis=-1))
    expo = jnp.where(visible, jnp.exp(scores - peak_next[..., None]), 0.0)
    summed_next = jnp.sum(expo, axis=-1)
    accum_next = jnp.einsum("schn,snhd->schd", expo, block_values.astype(jnp.float32))
    depth_ctx = (
        (accum_next / summed_next[..., None])
        .reshape(sess_rows, cb_local, depth_width)
        .astype(jnp.bfloat16)
    )
    projected = jnp.einsum("sce,cef->scf", depth_ctx, depth_out, preferred_element_type=jnp.float32)
    return (depth_in + projected).astype(jnp.bfloat16)


def solution(mesh):
    in_specs = (
        P(None, "sess"),
        P("sess", "tp", None),
        P("sess", None, "tp", None, None),
        P("sess"),
        P("tp", "sess"),
        P("sess"),
        P("tp", "sess", None),
        P("tp", "sess", None),
        P(None, "tp"),
        P("tp", None),
        P("tp", None, None),
        P("tp", None, None),
    )
    out_specs = P("sess", "tp", None)
    return jax.shard_map(shards, mesh=mesh, in_specs=in_specs, out_specs=out_specs, check_vma=False)
```

profile of v0, /device:TPU:0, one launch (start us, length us, event | category | flops | bytes accessed | tf_op | source)
XLA Modules:
  0.0 264.0 jit_solution(9343530428508861457)
XLA Ops:
  6.5 0.0 copy-start
  6.5 0.0 all-reduce.2.cloned.1.call-start
  6.5 0.9 slice_bitcast_fusion
  7.4 0.7 bitcast_convert_fusion
  8.2 0.7 iota_compare_fusion.1
  8.9 0.1 fusion.56
  9.0 0.0 copy-start.3
  9.0 3.6 %select_reduce_fusion = (f32[16,8]{1,0:T(8,128)S(1)}, f32[16,8,1024]{2,1,0:T(8,128)S(1)}) fusion(pred[16,1024]{1,0:T(8,128)(4,1)S(1)} %iota_compare_fusion.1, bf16[16,8,128]{2,1,0:T(8,128)(2,1)S(1)} %bitcast.122, bf16[16,2,1,1024,128]{4,3,2,1,0:T(8,128)(2,1)} %param.14), kind=kOutput, calls=%fused_computation.27 | convolution fusion | flops 33947520 | bytes 4768256 | tf_op jit(solution)/shard_map/skgd,skld->skgl/dot_general | solution.py:22
  12.6 0.0 copy-start.7
  12.6 0.0 copy-start.6
  12.6 0.3 fusion.41
  12.9 3.0 %fusion.33 = bf16[16,8,128]{2,1,0:T(8,128)(2,1)S(1)} fusion(bf16[16,2,1,1024,128]{4,3,2,1,0:T(8,128)(2,1)} %param.14, f32[16,8,1024]{2,1,0:T(8,128)S(1)} %get-tuple-element.12, f32[16,8]{1,0:T(8,128)S(1)} %get-tuple-element.10, f32[16,8]{1,0:T(8,128)S(1)} %multiply_maximum_fusion, pred[16,1024]{1,0:T(8,128)(4,1)S(1)} %iota_compare_fusion.1, ...), kind=kOutput, calls=%fused_computation.21 | convolution fusion | flops 34127872 | bytes 4777472 | tf_op jit(solution)/shard_map/skgl,skld->skgd/dot_general | solution.py:37
  16.0 22.5 %all_gather.6 = bf16[256,1024]{1,0:T(8,128)(2,1)S(1)} all-gather(bf16[16,1024]{1,0:T(8,128)(2,1)S(1)} %bitcast.123), channel_id=1, replica_groups=mesh['sess'=16,'tp'=8] {'sess'}, dimensions={0}, use_global_device_ids=true | all-gather | bytes 557056 | tf_op jit(solution)/shard_map/all_gather | solution.py:69
  38.5 0.0 copy-done.3
  38.5 1.2 fusion.62
  39.7 0.0 all-reduce.2.cloned.1.call-update
  39.7 0.0 reduce-scatter.2.cloned.1.call-start
  39.8 0.0 copy-done.7
  39.8 84.0 %all-reduce.2.cloned.1.call-done = f32[256,512]{1,0:T(8,128)} async-done(((f32[256,512]{1,0:T(8,128)}), f32[256,512]{1,0:T(8,128)}) %all-reduce.2.cloned.1.call-update) | async-done | bytes 524304 | tf_op jit(solution)/shard_map/psum | solution.py:73
  123.8 0.0 copy-done.2
  123.8 1.2 multiply_reduce_fusion
  125.0 27.1 %psum.15 = f32[256]{0:T(256)S(1)} all-reduce(f32[256]{0:T(256)S(1)} %multiply_reduce_fusion), channel_id=1, replica_groups=mesh['sess'=16,'tp'=8] {'sess'}, use_global_device_ids=true, to_apply=%region_4.5 | all-reduce | flops 256 | bytes 2048 | tf_op jit(solution)/shard_map/psum | solution.py:75
  152.2 0.0 copy-done.1
  152.2 0.0 copy-done.6
  152.2 1.5 convolution_bitcast_fusion.1
  153.7 2.3 fusion.17
  156.0 0.0 reduce-scatter.2.cloned.1.call-update
  156.0 57.4 %reduce-scatter.2.cloned.1.call-done = f32[16,1024]{1,0:T(8,128)} async-done(((f32[256,1024]{1,0:T(8,128)}), f32[16,1024]{1,0:T(8,128)}) %reduce-scatter.2.cloned.1.call-update) | async-done | bytes 65552 | tf_op jit(solution)/shard_map/reduce_scatter | solution.py:85
  213.4 1.0 multiply_reduce_fusion.1
  214.3 0.0 copy-done.5
  214.3 0.0 copy-start.4
  214.4 3.8 %fusion.11 = bf16[16,1,3072]{2,0,1:T(8,128)(2,1)S(1)} fusion(bf16[1,1024,3072]{2,1,0:T(8,128)(2,1)} %param.22, f32[16,1024]{1,0:T(8,128)} %reduce-scatter.2.cloned.1.call-done, f32[1024]{0:T(1024)S(1)} %bitcast.129, f32[16]{0:T(128)S(1)} %add_rsqrt_fusion.1), kind=kOutput, calls=%fused_computation.9 | convolution fusion | flops 100761600 | bytes 6459456 | tf_op jit(solution)/shard_map/sce,cef->scf/dot_general | solution.py:96
  218.2 35.2 %all_gather.7 = bf16[16,8,2048]{2,0,1:T(8,128)(2,1)S(1)} all-gather(bf16[16,1,2048]{2,0,1:T(8,128)(2,1)S(1)} %slice.36), channel_id=1, replica_groups=mesh['sess'=16,'tp'=8] {'tp'}, dimensions={1}, use_global_device_ids=true | all-gather | bytes 589824 | tf_op jit(solution)/shard_map/all_gather | solution.py:105
  253.5 0.3 reshape.256
  253.8 0.1 reshape.267
  254.0 0.5 fusion.39
  254.5 0.1 copy.25
  254.6 0.1 select_reduce_fusion.1
  254.7 0.1 fusion.52
  254.8 0.1 fusion.53
  254.9 0.1 copy.27
  255.0 0.3 reshape.255
  255.4 0.5 fusion.37
  255.9 0.1 divide_convert_fusion.2
  256.0 0.1 convert_element_type.66
  256.1 0.0 copy-done
  256.1 0.0 copy-done.4
  256.2 1.0 fusion.30
  (15 shorter events, 0.1 us)
Async XLA Ops:
  6.5 249.6 %copy-start = (bf16[1,1024,1024]{2,1,0:T(8,128)(2,1)S(1)}, bf16[1,1024,1024]{2,1,0:T(8,128)(2,1)}, u32[]{:S(2)}) copy-start(bf16[1,1024,1024]{2,1,0:T(8,128)(2,1)} %param.23) | copy-start | bytes 6291460
  6.5 117.3 %all-reduce.2.cloned.1.call-start = ((), (), s32[]{:S(2)}) async-start(), calls=%async_computation.1 | async-start | bytes 1048576 | tf_op jit(solution)/shard_map/psum | solution.py:73
  9.0 29.4 %copy-start.3 = (bf16[1024,512]{1,0:T(8,128)(2,1)S(1)}, bf16[1024,512]{1,0:T(8,128)(2,1)}, u32[]{:S(2)}) copy-start(bf16[1024,512]{1,0:T(8,128)(2,1)} %param.16) | copy-start | bytes 3145732
  12.6 27.2 %copy-start.7 = (s32[256,1]{0,1:T(1,128)S(1)}, s32[256,1]{0,1:T(1,128)}, u32[]{:S(2)}) copy-start(s32[256,1]{0,1:T(1,128)} %param.20) | copy-start | bytes 3076
  12.6 111.2 %copy-start.2 = (bf16[256,512]{1,0:T(8,128)(2,1)S(1)}, bf16[256,512]{1,0:T(8,128)(2,1)}, u32[]{:S(2)}) copy-start(bf16[256,512]{1,0:T(8,128)(2,1)} %param.12) | copy-start | bytes 786436
  12.6 139.6 %copy-start.1 = (bf16[1,512,1024]{2,1,0:T(8,128)(2,1)S(1)}, bf16[1,512,1024]{2,1,0:T(8,128)(2,1)}, u32[]{:S(2)}) copy-start(bf16[1,512,1024]{2,1,0:T(8,128)(2,1)} %param.18) | copy-start | bytes 3145732
  12.6 139.6 %copy-start.6 = (f32[512]{0:T(512)S(1)}, f32[512]{0:T(512)}, u32[]{:S(2)}) copy-start(f32[512]{0:T(512)} %param.17) | copy-start | bytes 6148
  16.0 198.4 %copy-start.5 = (f32[1,1024]{1,0:T(1,128)S(1)}, f32[1,1024]{1,0:T(1,128)}, u32[]{:S(2)}) copy-start(f32[1,1024]{1,0:T(1,128)} %param.21) | copy-start | bytes 12292
  39.7 173.6 %reduce-scatter.2.cloned.1.call-start = ((), (), s32[]{:S(2)}) async-start(), calls=%async_computation.2 | async-start | bytes 1114112 | tf_op jit(solution)/shard_map/reduce_scatter | solution.py:85
  214.3 41.8 %copy-start.4 = (f32[16,1024]{1,0:T(8,128)S(1)}, f32[16,1024]{1,0:T(8,128)}, u32[]{:S(2)}) copy-start(f32[16,1024]{1,0:T(8,128)} %reduce-scatter.2.cloned.1.call-done) | copy-start | bytes 196612
Sparse Core Ops, SparseCore 0:
  39.9 83.8 all-reduce.1
  156.1 57.2 reduce-scatter.1
where the time goes:
time: 264 us
  waiting for transfers between devices  141 us (53%)
  blocking collectives  84.9 us (32%)
  matrix products  17.6 us (7%)
  between operations  13.6 us (5%)
  other arithmetic  4.31 us (2%)
    psum x1, waiting for transfers between devices, shards(): summed = lax.psum(partial_out, 'tp')  84 us
    reduce_scatter x1, waiting for transfers between devices, shards(): lax.psum_scatter((projected + looked).reshape(sess_rows * lax.axis_size('...  57.4 us
    all_gather x1, blocking collectives, shards(): block_in = lax.all_gather(key_values, 'tp', axis=1, tiled=True)  35.2 us
    psum x1, blocking collectives, shards(): squares = lax.psum(jnp.sum(hidden * hidden, axis=1), 'sess')  27.1 us
    all_gather x1, blocking collectives, shards(): lax.all_gather(attn_rows, 'sess', axis=0, tiled=True)  22.5 us
  transfers between devices with their start and end apart: 2, of which 2 were waited for; matrix products, arithmetic and copies ran while one was open for 0% of the time, Pallas kernels for 0%

commit v1 on v0

--- a/solution.py
+++ b/solution.py
@@ -70,7 +70,7 @@
         wo_temporal,
         preferred_element_type=jnp.float32,
     )
-    summed = lax.psum(partial_out, "tp")
+    summed = jnp.sum(lax.all_gather(partial_out, "tp"), axis=0)
     hidden = x_resid.astype(jnp.float32) + summed
     squares = lax.psum(jnp.sum(hidden * hidden, axis=1), "sess")
     normed = normalize_rows(hidden, squares, norm_gain)

time: 264 us -> 254 us (0.962)
  waiting for transfers between devices: 141 us -> 128 us
    psum x1 -> x0, waiting for transfers between devices: 84 us -> none  [shards(): summed = lax.psum(partial_out, 'tp')]
    all_gather x0 -> x1, waiting for transfers between devices: none -> 70.2 us  [shards(): summed = jnp.sum(lax.all_gather(partial_out, 'tp'), axis=0)]
    reduce_sum x0 -> x1, other arithmetic: none -> 2.7 us  [shards(): summed = jnp.sum(lax.all_gather(partial_out, 'tp'), axis=0)]
where the time goes in v1:
time: 254 us
  waiting for transfers between devices  128 us (50%)
  blocking collectives  87 us (34%)
  matrix products  16.8 us (7%)
  between operations  13.6 us (5%)
  other arithmetic  5.98 us (2%)
    all_gather x1, waiting for transfers between devices, shards(): summed = jnp.sum(lax.all_gather(partial_out, 'tp'), axis=0)  70.2 us
    reduce_scatter x1, waiting for transfers between devices, shards(): lax.psum_scatter((projected + looked).reshape(sess_rows * lax.axis_size('...  58.1 us
    all_gather x1, blocking collectives, shards(): block_in = lax.all_gather(key_values, 'tp', axis=1, tiled=True)  35.2 us
    psum x1, blocking collectives, shards(): squares = lax.psum(jnp.sum(hidden * hidden, axis=1), 'sess')  29.1 us
    all_gather x1, blocking collectives, shards(): lax.all_gather(attn_rows, 'sess', axis=0, tiled=True)  22.6 us
  transfers between devices with their start and end apart: 2, of which 2 were waited for; matrix products, arithmetic and copies ran while one was open for 0% of the time, Pallas kernels for 0%

profile of v1, /device:TPU:0, one launch (start us, length us, event | category | flops | bytes accessed | tf_op | source)
XLA Modules:
  0.0 253.9 jit_solution(13949070060314164478)
XLA Ops:
  6.5 0.0 copy-start
  6.5 0.0 all-gather.3.cloned.1.call-start
  6.5 0.9 slice_bitcast_fusion
  7.4 0.7 bitcast_convert_fusion
  8.2 0.7 iota_compare_fusion.1
  8.9 0.1 fusion.56
  9.0 3.6 %select_reduce_fusion = (f32[16,8]{1,0:T(8,128)S(1)}, f32[16,8,1024]{2,1,0:T(8,128)S(1)}) fusion(pred[16,1024]{1,0:T(8,128)(4,1)S(1)} %iota_compare_fusion.1, bf16[16,8,128]{2,1,0:T(8,128)(2,1)S(1)} %bitcast.124, bf16[16,2,1,1024,128]{4,3,2,1,0:T(8,128)(2,1)} %param.14), kind=kOutput, calls=%fused_computation.27 | convolution fusion | flops 33947520 | bytes 4768256 | tf_op jit(solution)/shard_map/skgd,skld->skgl/dot_general | solution.py:22
  12.6 0.3 fusion.41
  12.9 0.0 copy-start.1
  12.9 0.0 copy-start.6
  12.9 3.0 %fusion.33 = bf16[16,8,128]{2,1,0:T(8,128)(2,1)S(1)} fusion(bf16[16,2,1,1024,128]{4,3,2,1,0:T(8,128)(2,1)} %param.14, f32[16,8,1024]{2,1,0:T(8,128)S(1)} %get-tuple-element.12, f32[16,8]{1,0:T(8,128)S(1)} %get-tuple-element.10, f32[16,8]{1,0:T(8,128)S(1)} %multiply_maximum_fusion, pred[16,1024]{1,0:T(8,128)(4,1)S(1)} %iota_compare_fusion.1, ...), kind=kOutput, calls=%fused_computation.21 | convolution fusion | flops 34127872 | bytes 4777472 | tf_op jit(solution)/shard_map/skgl,skld->skgd/dot_general | solution.py:37
  15.9 22.6 %all_gather.12 = bf16[256,1024]{1,0:T(8,128)(2,1)S(1)} all-gather(bf16[16,1024]{1,0:T(8,128)(2,1)S(1)} %bitcast.125), channel_id=1, replica_groups=mesh['sess'=16,'tp'=8] {'sess'}, dimensions={0}, use_global_device_ids=true | all-gather | bytes 557056 | tf_op jit(solution)/shard_map/all_gather | solution.py:69
  38.5 0.0 copy-done.2
  38.5 1.2 fusion.62
  39.8 0.0 all-gather.3.cloned.1.call-update
  39.8 0.0 reduce-scatter.2.cloned.1.call-start
  39.9 0.0 copy-done.7
  39.9 70.2 %all-gather.3.cloned.1.call-done = f32[2048,512]{1,0:T(8,128)} async-done(((f32[256,512]{1,0:T(8,128)}), f32[2048,512]{1,0:T(8,128)}) %all-gather.3.cloned.1.call-update) | async-done | bytes 4194320 | tf_op jit(solution)/shard_map/all_gather | solution.py:73
  110.1 2.7 %reduce_sum.46 = f32[256,512]{1,0:T(8,128)S(1)} reduce(f32[8,256,512]{2,1,0:T(8,128)} %bitcast.122, f32[]{:T(128)} %constant.5.clone.1), dimensions={0}, to_apply=%region_2.3 | reduce | flops 917504 | bytes 4718596 | tf_op jit(solution)/shard_map/reduce_sum | solution.py:73
  112.8 0.0 copy-done.1
  112.8 0.1 multiply_reduce_fusion
  113.0 29.1 %psum.7 = f32[256]{0:T(256)S(1)} all-reduce(f32[256]{0:T(256)S(1)} %multiply_reduce_fusion), channel_id=1, replica_groups=mesh['sess'=16,'tp'=8] {'sess'}, use_global_device_ids=true, to_apply=%region_4.5 | all-reduce | flops 256 | bytes 2048 | tf_op jit(solution)/shard_map/psum | solution.py:75
  142.1 0.0 copy-done.6
  142.1 1.7 convolution_bitcast_fusion.1
  143.8 0.0 copy-done.4
  143.8 1.3 fusion.17
  145.2 0.0 reduce-scatter.2.cloned.1.call-update
  145.2 58.1 %reduce-scatter.2.cloned.1.call-done = f32[16,1024]{1,0:T(8,128)} async-done(((f32[256,1024]{1,0:T(8,128)}), f32[16,1024]{1,0:T(8,128)}) %reduce-scatter.2.cloned.1.call-update) | async-done | bytes 65552 | tf_op jit(solution)/shard_map/reduce_scatter | solution.py:85
  203.3 1.0 multiply_reduce_fusion.1
  204.3 0.0 copy-done.5
  204.3 0.0 copy-start.3
  204.3 3.8 %fusion.11 = bf16[16,1,3072]{2,0,1:T(8,128)(2,1)S(1)} fusion(bf16[1,1024,3072]{2,1,0:T(8,128)(2,1)} %param.22, f32[16,1024]{1,0:T(8,128)} %reduce-scatter.2.cloned.1.call-done, f32[1024]{0:T(1024)S(1)} %bitcast.131, f32[16]{0:T(128)S(1)} %add_rsqrt_fusion.1), kind=kOutput, calls=%fused_computation.9 | convolution fusion | flops 100761600 | bytes 6459456 | tf_op jit(solution)/shard_map/sce,cef->scf/dot_general | solution.py:96
  208.2 35.2 %all_gather.15 = bf16[16,8,2048]{2,0,1:T(8,128)(2,1)S(1)} all-gather(bf16[16,1,2048]{2,0,1:T(8,128)(2,1)S(1)} %slice.36), channel_id=1, replica_groups=mesh['sess'=16,'tp'=8] {'tp'}, dimensions={1}, use_global_device_ids=true | all-gather | bytes 589824 | tf_op jit(solution)/shard_map/all_gather | solution.py:105
  243.4 0.3 reshape.256
  243.8 0.1 reshape.268
  243.9 0.5 fusion.39
  244.4 0.1 copy.25
  244.5 0.1 select_reduce_fusion.1
  244.6 0.1 fusion.52
  244.7 0.1 fusion.53
  244.8 0.1 copy.27
  244.9 0.3 reshape.255
  245.3 0.5 fusion.37
  245.8 0.1 divide_convert_fusion.2
  245.9 0.1 convert_element_type.66
  246.1 0.0 copy-done
  246.1 0.0 copy-done.3
  246.1 1.0 fusion.30
  (16 shorter events, 0.1 us)
Async XLA Ops:
  6.5 239.5 %copy-start = (bf16[1,1024,1024]{2,1,0:T(8,128)(2,1)S(1)}, bf16[1,1024,1024]{2,1,0:T(8,128)(2,1)}, u32[]{:S(2)}) copy-start(bf16[1,1024,1024]{2,1,0:T(8,128)(2,1)} %param.23) | copy-start | bytes 6291460
  6.5 103.6 %all-gather.3.cloned.1.call-start = ((), (), s32[]{:S(2)}) async-start(), calls=%async_computation.2 | async-start | bytes 4718592 | tf_op jit(solution)/shard_map/all_gather | solution.py:73
  9.0 29.5 %copy-start.2 = (bf16[1024,512]{1,0:T(8,128)(2,1)S(1)}, bf16[1024,512]{1,0:T(8,128)(2,1)}, u32[]{:S(2)}) copy-start(bf16[1024,512]{1,0:T(8,128)(2,1)} %param.16) | copy-start | bytes 3145732
  12.6 27.3 %copy-start.7 = (s32[256,1]{0,1:T(1,128)S(1)}, s32[256,1]{0,1:T(1,128)}, u32[]{:S(2)}) copy-start(s32[256,1]{0,1:T(1,128)} %param.20) | copy-start | bytes 3076
  12.9 99.9 %copy-start.1 = (bf16[256,512]{1,0:T(8,128)(2,1)S(1)}, bf16[256,512]{1,0:T(8,128)(2,1)}, u32[]{:S(2)}) copy-start(bf16[256,512]{1,0:T(8,128)(2,1)} %param.12) | copy-start | bytes 786436
  12.9 129.2 %copy-start.6 = (f32[512]{0:T(512)S(1)}, f32[512]{0:T(512)}, u32[]{:S(2)}) copy-start(f32[512]{0:T(512)} %param.17) | copy-start | bytes 6148
  15.9 127.9 %copy-start.4 = (bf16[1,128,1024]{2,1,0:T(8,128)(2,1)S(1)}, bf16[1,128,1024]{2,1,0:T(8,128)(2,1)}, u32[]{:S(2)}) copy-start(bf16[1,128,1024]{2,1,0:T(8,128)(2,1)} %param.19) | copy-start | bytes 786436
  39.8 164.5 %copy-start.5 = (f32[1,1024]{1,0:T(1,128)S(1)}, f32[1,1024]{1,0:T(1,128)}, u32[]{:S(2)}) copy-start(f32[1,1024]{1,0:T(1,128)} %param.21) | copy-start | bytes 12292
  39.8 163.5 %reduce-scatter.2.cloned.1.call-start = ((), (), s32[]{:S(2)}) async-start(), calls=%async_computation.1 | async-start | bytes 1114112 | tf_op jit(solution)/shard_map/reduce_scatter | solution.py:85
  204.3 41.8 %copy-start.3 = (f32[16,1024]{1,0:T(8,128)S(1)}, f32[16,1024]{1,0:T(8,128)}, u32[]{:S(2)}) copy-start(f32[16,1024]{1,0:T(8,128)} %reduce-scatter.2.cloned.1.call-done) | copy-start | bytes 196612
Sparse Core Ops, SparseCore 0:
  39.9 70.1 all-gather.2
  145.3 57.9 reduce-scatter.1
